TPU v7x, 32 devices: a whole 2x2x4 slice. The times are simulated.
32 devices in a mesh: elem: 32 (over z, y, x, core).
Axes of the slice: x: 2, y: 2, z: 4, core: 2. Of those that a mesh axis runs over, the one named last changes fastest.
Arguments:
- a_blocks: float32 [1024, 7, 4096], P('elem'), may hold values from -0.25 to 0.25
- p_blocks: float32 [1024, 2, 4096], P('elem'), may hold values from -1.2 to 1.2
- a_slot: int32 [1024, 7], P('elem'), may hold values from 0 to 93
- serve_rows: int32 [32, 31, 2], P('elem'), may hold values from 0 to 31
- row_count: int32 [32], P('elem'), may hold values from 8 to 32, as said below
- contrib_slot: int32 [1024, 28], P('elem'), may hold values from 0 to 127
- recv_tile: int32 [32, 32, 4], P('elem'), may hold values from 0 to 7
Outputs:
- coarse: float32 [256, 4096], P('elem')
Inputs may be any that keep to these rules, and one draw needn't show every extreme that they name: `row_count`: rows of a device at or beyond its count are padding and contribute nothing; some device has exactly 32.
All inputs are finite; a program needn't handle non-finite values.
Results may differ from a plain program's by a relative error of at most 0.0003.
Values sent between devices are 32-bit elements; how exact they have to be, the bound alone decides.
No kernel may reach another device: no remote copies, remote signals or barrier semaphores. Data moves between devices by JAX's collectives and lax.ppermute only.
A program may use at most 192 MiB of HBM per device.

v0:
```python
import functools

import jax
import jax.numpy as jnp
from jax import lax
from jax.experimental import pallas as pl
from jax.experimental.pallas import tpu as pltpu
from jax.sharding import PartitionSpec as P

B = 64
HALF = B // 2
LANES = 2 * B
TO = 8
UNROLL = 4
RING = 16
META = 8
VMEM_LIMIT = 56 * 1024 * 1024


def low_lanes(rows):
    return lax.broadcasted_iota(jnp.int32, (rows, LANES), 1) < B


def split_rows(value):
    high = value.astype(jnp.bfloat16)
    low = (value - high.astype(jnp.float32)).astype(jnp.bfloat16)
    return jnp.concatenate([high, high, low, low], axis=0)


def params(**more):
    return pltpu.CompilerParams(vmem_limit_bytes=VMEM_LIMIT, **more)


def prep_kernel(n, serve_count, me_ref, serve_ref, p_ref, own_out, send_out, own, sems, own_sem):
    rows = p_ref.shape[0]
    mask = low_lanes(HALF)

    def relayout(i, carry):
        first = p_ref[i, pl.ds(0, HALF, stride=2), :]
        second = p_ref[i, pl.ds(1, HALF, stride=2), :]
        own[i, pl.ds(0, HALF, stride=2), :] = jnp.where(mask, first, pltpu.roll(second, B, 1))
        own[i, pl.ds(1, HALF, stride=2), :] = jnp.where(mask, pltpu.roll(first, B, 1), second)
        return carry

    lax.fori_loop(0, rows, relayout, 0, unroll=4)
    me = me_ref[0]
    own_copy = pltpu.make_async_copy(own, own_out, own_sem)

    def copy(target, c, row):
        return pltpu.make_async_copy(own.at[row], send_out.at[target, c], sems.at[target, c])

    def send(target, carry):
        offset = target - me - 1
        offset = jnp.where(offset < 0, offset + n, offset)
        offset = jnp.minimum(offset, n - 2)
        for c in range(serve_count):
            copy(target, c, serve_ref[0, offset, c]).start()
        return carry

    def finish(target, carry):
        for c in range(serve_count):
            copy(target, c, 0).wait()
        return carry

    lax.fori_loop(0, n, send, 0)
    own_copy.start()
    lax.fori_loop(0, n, finish, 0)
    own_copy.wait()


def add_products(acc, out, dest):
    mask = low_lanes(B)
    for p in range(2):
        rows = out[p * B : (p + 1) * B]
        left = jnp.where(mask, rows, 0.0)
        acc[dest[2 * p]] += left
        acc[dest[2 * p + 1]] += rows - left


def fold(acc, slot):
    even = acc[slot, pl.ds(0, HALF, stride=2), :]
    odd = acc[slot, pl.ds(1, HALF, stride=2), :]
    even = even + pltpu.roll(even, B, 1)
    odd = odd + pltpu.roll(odd, B, 1)
    return jnp.where(low_lanes(HALF), even, odd)


def near_kernel(n, count_row, a_slot, contrib, me_ref, own_ref, a_ref, left_ref, slots_ref, meta_ref, acc, near_meta):
    step = pl.program_id(0)
    rows = own_ref.shape[0]
    blocks = a_ref.shape[1]
    slot_count = slots_ref.shape[0]
    per_row = contrib.shape[1] // 2

    @pl.when(step == 0)
    def start():
        acc[...] = jnp.zeros_like(acc)

    mask = low_lanes(HALF)
    y_even = own_ref[step, pl.ds(0, HALF, stride=2), :]
    y_odd = own_ref[step, pl.ds(1, HALF, stride=2), :]
    p_rows = jnp.concatenate([y_even, y_odd], axis=0)
    high = p_rows.astype(jnp.bfloat16).astype(jnp.float32)
    pair = jnp.concatenate([high, p_rows - high], axis=0).T.astype(jnp.bfloat16)
    lhs = jnp.concatenate([pair, pair], axis=1)
    for k in range(blocks):
        tile = a_ref[0, k]
        turned = pltpu.roll(tile, B, 1)
        both = jnp.concatenate([jnp.where(mask, tile, turned), jnp.where(mask, turned, tile)], axis=0)
        left = jnp.dot(lhs, split_rows(both), preferred_element_type=jnp.float32)
        left_high = left.astype(jnp.bfloat16).astype(jnp.float32)
        packed = jnp.where(low_lanes(2 * B), left_high, left - left_high)
        left_ref[step * blocks + k] = packed.astype(jnp.bfloat16)

    @pl.when(step == pl.num_programs(0) - 1)
    def own_products():
        me = me_ref[0]
        live = count_row[0]

        def put(ref, at, f, row, i, k):
            ref[at * META] = f
            ref[at * META + 1] = row
            for p in range(2):
                for q in range(2):
                    ref[at * META + 2 + 2 * p + q] = contrib[i, p * per_row + 2 * k + q]

        def put_pad(ref, at):
            ref[at * META] = 0
            ref[at * META + 1] = 0
            for j in range(4):
                ref[at * META + 2 + j] = slot_count

        def scan_row(i, carry):
            near_count, far_count = carry
            for k in range(blocks):
                slot = a_slot[i, k]
                is_near = slot < rows
                index = slot - rows
                source = me - 1 - index // 2
                source = jnp.where(source < 0, source + n, source)
                f = i * blocks + k
                put(near_meta, near_count, f, jnp.where(is_near, slot, 0), i, k)
                put(meta_ref, far_count, f, jnp.where(is_near, 0, source * 2 + index % 2), i, k)
                near_count = near_count + jnp.where(is_near, 1, 0)
                far_count = far_count + jnp.where(is_near, 0, 1)
            return near_count, far_count

        near_count, far_count = lax.fori_loop(0, jnp.minimum(live, rows), scan_row, (0, 0))
        for j in range(UNROLL):
            put_pad(near_meta, near_count + j)
            put_pad(meta_ref, far_count + j)
        meta_ref[meta_ref.shape[0] - 1] = far_count

        def products(g, carry):
            for u in range(UNROLL):
                at = (g * UNROLL + u) * META
                lp = left_ref[near_meta[at]]
                weights = split_rows(own_ref[near_meta[at + 1]])
                out = jnp.dot(jnp.concatenate([lp, lp], axis=1), weights, preferred_element_type=jnp.float32)
                add_products(acc, out, [near_meta[at + 2 + j] for j in range(4)])
            return carry

        lax.fori_loop(0, (near_count + UNROLL - 1) // UNROLL, products, 0)

        def pack(slot, carry):
            slots_ref[slot] = fold(acc, slot)
            return carry

        lax.fori_loop(0, slot_count, pack, 0, unroll=2)


def far_kernel(n, cap, me_ref, meta, left_hbm, recv_hbm, near_hbm, send_hbm, acc, recv, near, packed, ring, ring_sems, sems, out_sems):
    me = me_ref[0]
    slot_count = near.shape[0]
    recv_copy = pltpu.make_async_copy(recv_hbm, recv, sems.at[0])
    near_copy = pltpu.make_async_copy(near_hbm, near, sems.at[1])
    recv_copy.start()
    count = meta[meta.shape[0] - 1]
    groups = (count + UNROLL - 1) // UNROLL
    depth = RING // UNROLL

    def left_copy(entry, buffer):
        return pltpu.make_async_copy(left_hbm.at[meta[entry * META]], ring.at[buffer], ring_sems.at[buffer])

    def fetch(g):
        @pl.when(g < groups)
        def go():
            for u in range(UNROLL):
                left_copy(g * UNROLL + u, lax.rem(g, depth) * UNROLL + u).start()

    for g in range(depth - 1):
        fetch(g)
    near_copy.start()
    acc[...] = jnp.zeros_like(acc)
    recv_copy.wait()

    def products(g, carry):
        fetch(g + depth - 1)
        for u in range(UNROLL):
            left_copy(0, lax.rem(g, depth) * UNROLL + u).wait()
        for u in range(UNROLL):
            at = (g * UNROLL + u) * META
            lp = ring[lax.rem(g, depth) * UNROLL + u]
            weights = split_rows(recv[meta[at + 1]])
            out = jnp.dot(jnp.concatenate([lp, lp], axis=1), weights, preferred_element_type=jnp.float32)
            add_products(acc, out, [meta[at + 2 + j] for j in range(4)])
        return carry

    lax.fori_loop(0, groups, products, 0)
    near_copy.wait()

    def out_copy(m):
        owner = me + m
        owner = jnp.where(owner >= n, owner - n, owner)
        return pltpu.make_async_copy(packed.at[m], send_hbm.at[owner], out_sems.at[m])

    def pack(m, carry):
        for c in range(cap):
            slot = m * cap + c
            packed[m, c] = fold(acc, slot) + near[slot]
        out_copy(m).start()
        return carry

    lax.fori_loop(0, n, pack, 0)

    def finish(m, carry):
        out_copy(m).wait()
        return carry

    lax.fori_loop(0, n, finish, 0)


def final_kernel(n, cap, me_ref, tile_ref, got_ref, out_ref, total):
    me = me_ref[0]
    total[...] = jnp.zeros_like(total)

    def add(source, carry):
        m = me - source
        m = jnp.where(m < 0, m + n, m)
        for c in range(cap):
            rows = pl.ds(pl.multiple_of(tile_ref[0, m, c] * HALF, HALF), HALF)
            total[rows, :] += got_ref[source, c]
        return carry

    lax.fori_loop(0, n, add, 0)
    for r in range(HALF):
        out_ref[:, r * LANES : (r + 1) * LANES] = total[pl.ds(r, TO, stride=HALF), :]


def spec(space):
    return pl.BlockSpec(memory_space=space)


def body(a_blocks, p_blocks, a_slot, serve_rows, row_count, contrib_slot, recv_tile):
    n = lax.axis_size("elem")
    rows, blocks, _ = a_blocks.shape
    cap = recv_tile.shape[2]
    serve_count = serve_rows.shape[2]
    f32, i32, bf16 = jnp.float32, jnp.int32, jnp.bfloat16
    smem, vmem, hbm = spec(pltpu.SMEM), spec(pltpu.VMEM), spec(pl.ANY)
    me = lax.axis_index("elem").astype(i32).reshape(1)
    shape = jax.ShapeDtypeStruct

    p_view = p_blocks.reshape(rows, 2, HALF, LANES).transpose(0, 2, 1, 3).reshape(rows, B, LANES)
    own, send = pl.pallas_call(
        functools.partial(prep_kernel, n, serve_count),
        out_shape=(shape((rows, B, LANES), f32), shape((n, serve_count, B, LANES), f32)),
        in_specs=[smem, smem, vmem],
        out_specs=(hbm, hbm),
        scratch_shapes=[
            pltpu.VMEM((rows, B, LANES), f32),
            pltpu.SemaphoreType.DMA((n, serve_count)),
            pltpu.SemaphoreType.DMA,
        ],
        compiler_params=params(),
        name="prep",
    )(me, serve_rows, p_view)

    recv = lax.all_to_all(
        send.reshape(n, serve_count * B, LANES), "elem", split_axis=0, concat_axis=0, tiled=True
    ).reshape(n * serve_count, B, LANES)

    entries = rows * blocks
    slot_count = n * cap
    meta_size = (entries + 2 * UNROLL) * META
    a_tiles = a_blocks.reshape(rows, blocks, HALF, LANES)
    left, near_slots, meta = pl.pallas_call(
        functools.partial(near_kernel, n),
        grid=(rows,),
        out_shape=(
            shape((entries, 2 * B, LANES), bf16),
            shape((slot_count, HALF, LANES), f32),
            shape((meta_size,), i32),
        ),
        in_specs=[
            smem,
            smem,
            smem,
            smem,
            pl.BlockSpec((rows, B, LANES), lambda i: (0, 0, 0)),
            pl.BlockSpec((1, blocks, HALF, LANES), lambda i: (i, 0, 0, 0)),
        ],
        out_specs=(
            pl.BlockSpec((entries, 2 * B, LANES), lambda i: (0, 0, 0)),
            pl.BlockSpec((slot_count, HALF, LANES), lambda i: (0, 0, 0)),
            smem,
        ),
        scratch_shapes=[pltpu.VMEM((slot_count + 1, B, LANES), f32), pltpu.SMEM((meta_size,), i32)],
        compiler_params=params(dimension_semantics=("arbitrary",)),
        cost_estimate=pl.CostEstimate(flops=8 * entries * 2 * B * LANES * LANES, bytes_accessed=16 << 20, transcendentals=0),
        name="near",
    )(row_count, a_slot, contrib_slot, me, own, a_tiles)

    send_two = pl.pallas_call(
        functools.partial(far_kernel, n, cap),
        out_shape=shape((n, cap, HALF, LANES), f32),
        in_specs=[smem, smem, hbm, hbm, hbm],
        out_specs=hbm,
        scratch_shapes=[
            pltpu.VMEM((slot_count + 1, B, LANES), f32),
            pltpu.VMEM((n * serve_count, B, LANES), f32),
            pltpu.VMEM((slot_count, HALF, LANES), f32),
            pltpu.VMEM((n, cap, HALF, LANES), f32),
            pltpu.VMEM((RING, 2 * B, LANES), bf16),
            pltpu.SemaphoreType.DMA((RING,)),
            pltpu.SemaphoreType.DMA((2,)),
            pltpu.SemaphoreType.DMA((n,)),
        ],
        compiler_params=params(),
        cost_estimate=pl.CostEstimate(flops=4 * entries * 2 * B * LANES * LANES, bytes_accessed=16 << 20, transcendentals=0),
        name="far",
    )(me, meta, left, recv, near_slots)

    got = lax.all_to_all(
        send_two.reshape(n, cap * HALF, LANES), "elem", split_axis=0, concat_axis=0, tiled=True
    ).reshape(n, cap, HALF, LANES)

    return pl.pallas_call(
        functools.partial(final_kernel, n, cap),
        out_shape=shape((TO, B * B), f32),
        in_specs=[smem, smem, vmem],
        out_specs=vmem,
        scratch_shapes=[pltpu.VMEM((TO * HALF, LANES), f32)],
        compiler_params=params(),
        name="final",
    )(me, recv_tile, got)


def solution(mesh):
    in_specs = (
        P("elem", None, None),
        P("elem", None, None),
        P("elem", None),
        P("elem", None, None),
        P("elem"),
        P("elem", None),
        P("elem", None, None),
    )
    out_specs = P("elem", None)
    return jax.shard_map(body, mesh=mesh, in_specs=in_specs, out_specs=out_specs, check_vma=False)
```

profile of v0, /device:TPU:0, one launch (start us, length us, event | category | flops | bytes accessed | tf_op | source)
XLA Modules:
  0.0 137.4 jit_solution(13759373848602649717)
XLA Ops:
  0.0 1.4 copy.14.serve_ref
  1.4 4.3 %prep.1 = (f32[32,64,128]{2,1,0:T(8,128)}, f32[32,2,64,128]{3,2,1,0:T(8,128)}) custom-call(s32[1]{0:T(128)} %bitcast.me_ref, s32[1,31,2]{2,1,0:T(8,128)} %copy.14.serve_ref, f32[32,64,128]{2,1,0:T(8,128)} %bitcast.22), custom_call_target="tpu_custom_call" | custom-call | tf_op jit(solution)/shard_map/prep/pallas_call | solution.py:265
  5.6 7.3 %all-to-all-start = ((f32[32,128,128]{2,1,0:T(8,128)}), f32[32,128,128]{2,1,0:T(8,128)S(1)}, u32[]{:S(2)}, u32[]{:S(2)}) async-start(f32[32,128,128]{2,1,0:T(8,128)} %bitcast.21), calls=%async_computation | async-start | bytes 4194304 | tf_op jit(solution)/shard_map/all_to_all | solution.py:279
  13.0 2.7 %copy.18 = f32[28,8,32,128]{3,2,1,0:T(8,128)S(1)} copy(f32[28,8,32,128]{3,1,2,0:T(8,128)} %bitcast.20) | data formatting | bytes 7340032
  15.6 0.0 copy-start.2
  15.7 2.3 %copy.16.a_ref = f32[32,7,32,128]{3,2,1,0:T(8,128)} copy(f32[32,7,32,128]{3,2,0,1:T(8,128)S(1)} %bitcast.16) | data formatting | bytes 7340032 | tf_op jit(solution)/shard_map/reshape | solution.py:286
  18.0 0.0 copy-done.2
  18.0 0.7 copy.15.a_slot
  19.3 42.5 %near.1 = (bf16[224,128,128]{2,1,0:T(8,128)(2,1)}, f32[128,32,128]{2,1,0:T(8,128)}, s32[1856]{0:T(1024)}) custom-call(s32[1]{0:T(128)S(6)} %copy.19.count_row, s32[32,7]{1,0:T(8,128)} %copy.15.a_slot, s32[32,28]{1,0:T(8,128)} %contrib.1, s32[1]{0:T(128)} %bitcast.me_ref, f32[32,64,128]{2,1,0:T(8,128)} %get-tuple-element.10.own_ref, ...), custom_call_target="tpu_custom_call" | custom-call | flops 3758096384 | bytes 16777216 | tf_op jit(solution)/shard_map/near/pallas_call | solution.py:287
  61.8 0.0 all-to-all-done
  61.9 0.0 copy-start.1
  61.9 1.3 copy-done.1
  63.2 15.5 %far.1 = f32[32,4,32,128]{3,2,1,0:T(8,128)} custom-call(s32[1]{0:T(128)} %bitcast.me_ref, s32[1856]{0:T(1024)} %get-tuple-element.11.meta, bf16[224,128,128]{2,1,0:T(8,128)(2,1)} %get-tuple-element.12.left_hbm, f32[64,64,128]{2,1,0:T(8,128)} %bitcast.18, f32[128,32,128]{2,1,0:T(8,128)} %get-tuple-element.14.near_hbm), custom_call_target="tpu_custom_call" | custom-call | flops 1879048192 | bytes 16777216 | tf_op jit(solution)/shard_map/far/pallas_call | solution.py:314
  78.7 0.0 copy-start.3
  78.7 5.5 %all-to-all-start.1 = ((f32[32,128,128]{2,1,0:T(8,128)}), f32[32,128,128]{2,1,0:T(8,128)S(1)}, u32[]{:S(2)}, u32[]{:S(2)}) async-start(f32[32,128,128]{2,1,0:T(8,128)} %bitcast.19), calls=%async_computation.1 | async-start | bytes 4194304 | tf_op jit(solution)/shard_map/all_to_all | solution.py:334
  84.2 0.0 copy-done.3
  84.2 0.7 copy.17.tile_ref
  84.9 48.2 %all-to-all-done.1 = f32[32,128,128]{2,1,0:T(8,128)S(1)} async-done(((f32[32,128,128]{2,1,0:T(8,128)}), f32[32,128,128]{2,1,0:T(8,128)S(1)}, u32[]{:S(2)}, u32[]{:S(2)}) %all-to-all-start.1) | async-done | bytes 2097184 | tf_op jit(solution)/shard_map/all_to_all | solution.py:334
  133.1 0.0 copy-start
  133.1 1.3 copy-done
  134.5 3.0 %final.1 = f32[8,4096]{1,0:T(8,128)} custom-call(s32[1]{0:T(128)} %bitcast.me_ref, s32[1,32,4]{2,1,0:T(8,128)} %copy.17.tile_ref, f32[32,4,32,128]{3,2,1,0:T(8,128)} %bitcast.17), custom_call_target="tpu_custom_call" | custom-call | tf_op jit(solution)/shard_map/final/pallas_call | solution.py:338
Async XLA Ops:
  5.6 56.2 %all-to-all-start = ((f32[32,128,128]{2,1,0:T(8,128)}), f32[32,128,128]{2,1,0:T(8,128)S(1)}, u32[]{:S(2)}, u32[]{:S(2)}) async-start(f32[32,128,128]{2,1,0:T(8,128)} %bitcast.21), calls=%async_computation | async-start | bytes 4194304 | tf_op jit(solution)/shard_map/all_to_all | solution.py:279
  15.6 2.3 %copy-start.2 = (s32[32,7]{0,1:T(8,128)S(1)}, s32[32,7]{0,1:T(8,128)}, u32[]{:S(2)}) copy-start(s32[32,7]{0,1:T(8,128)} %param.9) | copy-start | bytes 2692
  61.9 1.3 copy-start.1
  78.7 5.6 %copy-start.3 = (s32[1,32,4]{1,2,0:T(4,128)S(1)}, s32[1,32,4]{1,2,0:T(4,128)}, u32[]{:S(2)}) copy-start(s32[1,32,4]{1,2,0:T(4,128)} %param.13) | copy-start | bytes 1540
  78.7 54.4 %all-to-all-start.1 = ((f32[32,128,128]{2,1,0:T(8,128)}), f32[32,128,128]{2,1,0:T(8,128)S(1)}, u32[]{:S(2)}, u32[]{:S(2)}) async-start(f32[32,128,128]{2,1,0:T(8,128)} %bitcast.19), calls=%async_computation.1 | async-start | bytes 4194304 | tf_op jit(solution)/shard_map/all_to_all | solution.py:334
  133.1 1.3 copy-start
where the time goes:
time: 139 us; the launch traced here: 137 us
  Pallas kernels  65.2 us (47%)
  waiting for transfers between devices  48.2 us (35%)
  starting transfers between devices  12.8 us (9%)
  local copies, waits for them, and re-layouts  10.4 us (7%)
    all_to_all x1, waiting for transfers between devices, body(): lax.all_to_all(send_two.reshape(n, cap * HALF, LANES), 'elem', split_axis...  48.2 us
    pallas_call x1, Pallas kernels, body(): pl.pallas_call(functools.partial(near_kernel, n), grid=(rows,), out_shape...  42.5 us
    pallas_call x1, Pallas kernels, body(): pl.pallas_call(functools.partial(far_kernel, n, cap), out_shape=shape((n,...  15.5 us
    unnamed x12, local copies, waits for them, and re-layouts  8.09 us
    all_to_all x1, starting transfers between devices, body(): lax.all_to_all(send.reshape(n, serve_count * B, LANES), 'elem', split_axi...  7.3 us
    all_to_all x1, starting transfers between devices, body(): lax.all_to_all(send_two.reshape(n, cap * HALF, LANES), 'elem', split_axis...  5.53 us
    pallas_call x1, Pallas kernels, body(): pl.pallas_call(functools.partial(prep_kernel, n, serve_count), out_shape=...  4.27 us
    pallas_call x1, Pallas kernels, body(): pl.pallas_call(functools.partial(final_kernel, n, cap), out_shape=shape((...  2.96 us
  transfers between devices with their start and end apart: 2, of which 1 were waited for; matrix products, arithmetic and copies ran while one was open for 5% of the time, Pallas kernels for 31%

commit v1 on v0

v1 whole, which is shorter than its diff:
```python
import functools

import jax
import jax.numpy as jnp
from jax import lax
from jax.experimental import pallas as pl
from jax.experimental.pallas import tpu as pltpu
from jax.sharding import PartitionSpec as P

B = 64
HALF = B // 2
LANES = 2 * B
TO = 8
PLACES = 4
GROUP = 2 * PLACES
CHUNKS = 4
RING = 16
UNROLL = 4
META = 8
MIB = 1 << 20


def low_lanes(rows):
    return lax.broadcasted_iota(jnp.int32, (rows, LANES), 1) < B


def split_rows(value):
    high = value.astype(jnp.bfloat16)
    low = (value - high.astype(jnp.float32)).astype(jnp.bfloat16)
    return jnp.concatenate([high, high, low, low], axis=0)


def params(mib, **more):
    return pltpu.CompilerParams(vmem_limit_bytes=mib * MIB, **more)


def prep_kernel(n, me_ref, serve_hbm, p_hbm, own, send_hbm, p_ref, serve_ref, p_sems, serve_sem, send_sem):
    rows = p_ref.shape[0]
    serve_count = serve_ref.shape[0]
    mask = low_lanes(HALF)
    chunk = rows // CHUNKS

    def chunk_copy(i):
        part = pl.ds(i * chunk, chunk)
        return pltpu.make_async_copy(p_hbm.at[part], p_ref.at[part], p_sems.at[i])

    serve_copy = pltpu.make_async_copy(serve_hbm, serve_ref, serve_sem)
    for i in range(CHUNKS):
        chunk_copy(i).start()
    serve_copy.start()

    def relayout(i, carry):
        first = p_ref[i, pl.ds(0, HALF, stride=2), :]
        second = p_ref[i, pl.ds(1, HALF, stride=2), :]
        turned = pltpu.roll(jnp.where(mask, second, first), B, 1)
        own[i, pl.ds(0, HALF, stride=2), :] = jnp.where(mask, first, turned)
        own[i, pl.ds(1, HALF, stride=2), :] = jnp.where(mask, turned, second)
        return carry

    for i in range(CHUNKS):
        chunk_copy(i).wait()
        lax.fori_loop(i * chunk, (i + 1) * chunk, relayout, 0, unroll=4)
    serve_copy.wait()
    me = me_ref[0]

    def serve(target, carry):
        offset = target - me - 1
        offset = jnp.where(offset < 0, offset + n, offset)
        offset = jnp.minimum(offset, n - 2)
        for c in range(serve_count):
            pltpu.make_async_copy(own.at[serve_ref[c, offset]], send_hbm.at[target, c], send_sem).start()
        return carry

    lax.fori_loop(0, n, serve, 0, unroll=4)
    pltpu.make_async_copy(send_hbm, send_hbm, send_sem).wait()


def add_products(acc, out, dest):
    mask = low_lanes(B)
    for p in range(2):
        rows = out[p * B : (p + 1) * B]
        left = jnp.where(mask, rows, 0.0)
        acc[dest[2 * p]] += left
        acc[dest[2 * p + 1]] += rows - left


def fold(acc, slot):
    mask = low_lanes(HALF)
    even = acc[slot, pl.ds(0, HALF, stride=2), :]
    odd = acc[slot, pl.ds(1, HALF, stride=2), :]
    return jnp.where(mask, even, odd) + pltpu.roll(jnp.where(mask, odd, even), B, 1)


def near_kernel(
    n, count_row, a_slot, contrib, me_ref, own_ref, a_ref, left_hbm, slots_hbm, meta_ref, acc, left_ref, slots_ref, near_meta, sems
):
    step = pl.program_id(0)
    rows = own_ref.shape[0]
    blocks = a_ref.shape[1]
    slot_count = slots_ref.shape[0]
    per_row = contrib.shape[1] // 2

    @pl.when(step == 0)
    def start():
        acc[...] = jnp.zeros_like(acc)

    mask = low_lanes(HALF)
    y_even = own_ref[step, pl.ds(0, HALF, stride=2), :]
    y_odd = own_ref[step, pl.ds(1, HALF, stride=2), :]
    p_rows = jnp.concatenate([y_even, y_odd], axis=0)
    high = p_rows.astype(jnp.bfloat16).astype(jnp.float32)
    pair = jnp.concatenate([high, p_rows - high], axis=0).T.astype(jnp.bfloat16)
    lhs = jnp.concatenate([pair, pair], axis=1)
    for k in range(blocks):
        tile = a_ref[0, k]
        turned = pltpu.roll(tile, B, 1)
        both = jnp.concatenate([jnp.where(mask, tile, turned), jnp.where(mask, turned, tile)], axis=0)
        left = jnp.dot(lhs, split_rows(both), preferred_element_type=jnp.float32)
        left_high = left.astype(jnp.bfloat16).astype(jnp.float32)
        packed = jnp.where(low_lanes(2 * B), left_high, left - left_high)
        left_ref[step * blocks + k] = packed.astype(jnp.bfloat16)
    part = pl.ds(step * blocks, blocks)
    pltpu.make_async_copy(left_ref.at[part], left_hbm.at[part], sems.at[0]).start()

    @pl.when(step == pl.num_programs(0) - 1)
    def own_products():
        me = me_ref[0]
        live = count_row[0]

        def put(ref, at, f, row, i, k):
            ref[at * META] = f
            ref[at * META + 1] = row
            for p in range(2):
                for q in range(2):
                    ref[at * META + 2 + 2 * p + q] = contrib[i, p * per_row + 2 * k + q]

        def put_pad(ref, at):
            ref[at * META] = 0
            ref[at * META + 1] = 0
            for j in range(4):
                ref[at * META + 2 + j] = slot_count

        def scan_row(i, carry):
            near_count, far_count = carry
            for k in range(blocks):
                slot = a_slot[k, i]
                is_near = slot < rows
                index = slot - rows
                source = me - 1 - index // 2
                source = jnp.where(source < 0, source + n, source)
                f = i * blocks + k
                put(near_meta, near_count, f, jnp.where(is_near, slot, 0), i, k)
                put(meta_ref, far_count, f, jnp.where(is_near, 0, source * 2 + index % 2), i, k)
                near_count = near_count + jnp.where(is_near, 1, 0)
                far_count = far_count + jnp.where(is_near, 0, 1)
            return near_count, far_count

        near_count, far_count = lax.fori_loop(0, jnp.minimum(live, rows), scan_row, (0, 0))
        for j in range(UNROLL):
            put_pad(near_meta, near_count + j)
            put_pad(meta_ref, far_count + j)
        meta_ref[meta_ref.shape[0] - 1] = far_count

        def products(g, carry):
            for u in range(UNROLL):
                at = (g * UNROLL + u) * META
                lp = left_ref[near_meta[at]]
                weights = split_rows(own_ref[near_meta[at + 1]])
                out = jnp.dot(jnp.concatenate([lp, lp], axis=1), weights, preferred_element_type=jnp.float32)
                add_products(acc, out, [near_meta[at + 2 + j] for j in range(4)])
            return carry

        lax.fori_loop(0, (near_count + UNROLL - 1) // UNROLL, products, 0)

        def pack(slot, carry):
            slots_ref[slot] = fold(acc, slot)
            return carry

        lax.fori_loop(0, slot_count, pack, 0, unroll=2)
        slots_copy = pltpu.make_async_copy(slots_ref, slots_hbm, sems.at[1])
        slots_copy.start()
        pltpu.make_async_copy(left_hbm, left_hbm, sems.at[0]).wait()
        slots_copy.wait()


def far_kernel(n, cap, me_ref, meta, left_hbm, recv, near_hbm, *refs):
    far_slots, own_slots = refs[:PLACES], refs[PLACES : 2 * PLACES]
    acc, near, ring, ring_sems, near_sem = refs[2 * PLACES :]
    me = me_ref[0]
    count = meta[meta.shape[0] - 1]
    turns = (count + UNROLL - 1) // UNROLL
    depth = RING // UNROLL

    def fetch(g):
        @pl.when(g < turns)
        def go():
            for u in range(UNROLL):
                buffer = lax.rem(g, depth) * UNROLL + u
                source = left_hbm.at[meta[(g * UNROLL + u) * META]]
                pltpu.make_async_copy(source, ring.at[buffer], ring_sems.at[buffer]).start()

    for g in range(depth - 1):
        fetch(g)
    near_copy = pltpu.make_async_copy(near_hbm, near, near_sem)
    near_copy.start()
    acc[...] = jnp.zeros_like(acc)

    def products(g, carry):
        fetch(g + depth - 1)
        for u in range(UNROLL):
            buffer = lax.rem(g, depth) * UNROLL + u
            pltpu.make_async_copy(left_hbm.at[0], ring.at[buffer], ring_sems.at[buffer]).wait()
        for u in range(UNROLL):
            at = (g * UNROLL + u) * META
            lp = ring[lax.rem(g, depth) * UNROLL + u]
            weights = split_rows(recv[meta[at + 1]])
            out = jnp.dot(jnp.concatenate([lp, lp], axis=1), weights, preferred_element_type=jnp.float32)
            add_products(acc, out, [meta[at + 2 + j] for j in range(4)])
        return carry

    lax.fori_loop(0, turns, products, 0)
    near_copy.wait()
    groups = n // GROUP
    place = lax.rem(me // 2, PLACES)
    group = me // GROUP

    def pack(j, step, target):
        at = group + step
        at = jnp.where(at >= groups, at - groups, at)
        for core in range(2):
            m = at * GROUP + (place ^ j) * 2 + core - me
            m = jnp.where(m < 0, m + n, m)
            for c in range(cap):
                slot = m * cap + c
                target[core, c] = fold(acc, slot) + near[slot]

    for j in range(PLACES):
        lax.fori_loop(1, groups, lambda step, carry, j=j: pack(j, step, far_slots[j].at[step - 1]) or carry, 0)
        pack(j, 0, own_slots[j])


def combine_kernel(n, cap, first, count, me_ref, table, *refs):
    slots, (mine, other) = refs[:PLACES], refs[PLACES:]
    groups = n // GROUP
    me = me_ref[0]
    core = lax.rem(me, 2)
    group = me // GROUP

    def gather(step, carry):
        at = group + first + step
        at = jnp.where(at >= groups, at - groups, at)
        for target, side in ((mine, core), (other, 1 - core)):
            entry = (at ^ group) * 2 + (side ^ core)
            target[step] = jnp.zeros_like(target[step])
            for j in range(PLACES):
                m = at * GROUP + side - (group * GROUP + core) - ((place_of(me) ^ j) - place_of(me)) * 2
                m = jnp.where(m < 0, m + n, m)
                m = jnp.where(m >= n, m - n, m)
                for c in range(cap):
                    target[step, table[entry * cap + c, m]] += slots[j][step, side, c]
        return carry

    lax.fori_loop(0, count, gather, 0)


def place_of(me):
    return lax.rem(me // 2, PLACES)


def final_kernel(*refs):
    parts, out_ref, total = refs[:-2], refs[-2], refs[-1]
    value = parts[0][...]
    for part in parts[1:]:
        value = value + part[...]
    total[...] = value.reshape(TO * HALF, LANES)
    for r in range(HALF):
        out_ref[:, r * LANES : (r + 1) * LANES] = total[pl.ds(r, TO, stride=HALF), :]


def spec(space):
    return pl.BlockSpec(memory_space=space)


def body(a_blocks, p_blocks, a_slot, serve_rows, row_count, contrib_slot, recv_tile):
    n = lax.axis_size("elem")
    rows, blocks, _ = a_blocks.shape
    cap = recv_tile.shape[2]
    serve_count = serve_rows.shape[2]
    f32, i32, bf16 = jnp.float32, jnp.int32, jnp.bfloat16
    smem, vmem, hbm = spec(pltpu.SMEM), spec(pltpu.VMEM), spec(pl.ANY)
    pinned = n <= 32
    me = lax.axis_index("elem").astype(i32).reshape(1)

    def shape(dims, dtype):
        return pltpu.VMEM(dims, dtype) if pinned else jax.ShapeDtypeStruct(dims, dtype)

    def pin(value):
        return pltpu.with_memory_space_constraint(value, pltpu.VMEM) if pinned else value

    def pin_hbm(value):
        return pltpu.with_memory_space_constraint(value, pltpu.HBM)

    def across(value, partner):
        return lax.ppermute(value, "elem", [(i, partner(i)) for i in range(n)])

    p_view = p_blocks.reshape(rows, 2, HALF, LANES).transpose(0, 2, 1, 3).reshape(rows, B, LANES)
    own, send = pl.pallas_call(
        functools.partial(prep_kernel, n),
        out_shape=(shape((rows, B, LANES), f32), pltpu.HBM((n, serve_count, B, LANES), f32)),
        in_specs=[smem, hbm, hbm],
        out_specs=(vmem, hbm),
        scratch_shapes=[
            pltpu.VMEM((rows, B, LANES), f32),
            pltpu.SMEM((serve_count, n - 1), i32),
            pltpu.SemaphoreType.DMA((CHUNKS,)),
            pltpu.SemaphoreType.DMA,
            pltpu.SemaphoreType.DMA,
        ],
        compiler_params=params(8),
        name="prep",
    )(me, pin_hbm(serve_rows[0].T), pin_hbm(p_view))

    recv = lax.all_to_all(
        send.reshape(n, serve_count * B, LANES), "elem", split_axis=0, concat_axis=0, tiled=True
    ).reshape(n * serve_count, B, LANES)

    table = recv_tile.transpose(0, 2, 1)
    for flip in [1] + [GROUP << i for i in range((n // GROUP).bit_length() - 1)]:
        table = jnp.concatenate([table, across(table, lambda i, flip=flip: i ^ flip)], axis=0)
    table = table.reshape(n // PLACES * cap, n)

    entries = rows * blocks
    slot_count = n * cap
    meta_size = (entries + 2 * UNROLL) * META
    a_tiles = a_blocks.reshape(rows, blocks, HALF, LANES)
    left, near_slots, meta = pl.pallas_call(
        functools.partial(near_kernel, n),
        grid=(rows,),
        out_shape=(
            pltpu.HBM((entries, 2 * B, LANES), bf16),
            pltpu.HBM((slot_count, HALF, LANES), f32),
            jax.ShapeDtypeStruct((meta_size,), i32),
        ),
        in_specs=[smem, smem, smem, smem, vmem, pl.BlockSpec((1, blocks, HALF, LANES), lambda i: (i, 0, 0, 0))],
        out_specs=(hbm, hbm, smem),
        scratch_shapes=[
            pltpu.VMEM((slot_count + 1, B, LANES), f32),
            pltpu.VMEM((entries, 2 * B, LANES), bf16),
            pltpu.VMEM((slot_count, HALF, LANES), f32),
            pltpu.SMEM((meta_size,), i32),
            pltpu.SemaphoreType.DMA((2,)),
        ],
        compiler_params=params(20 + n // 4, dimension_semantics=("arbitrary",)),
        cost_estimate=pl.CostEstimate(flops=8 * entries * 2 * B * LANES * LANES, bytes_accessed=16 << 20, transcendentals=0),
        name="near",
    )(row_count, a_slot.T, contrib_slot, me, pin(own), a_tiles)

    groups = n // GROUP
    slot_shapes = [shape((groups - 1, 2, cap, HALF, LANES), f32)] * PLACES + [shape((2, cap, HALF, LANES), f32)] * PLACES
    slots = pl.pallas_call(
        functools.partial(far_kernel, n, cap),
        out_shape=slot_shapes,
        in_specs=[smem, smem, hbm, vmem, hbm],
        out_specs=[vmem] * (2 * PLACES),
        scratch_shapes=[
            pltpu.VMEM((slot_count + 1, B, LANES), f32),
            pltpu.VMEM((slot_count, HALF, LANES), f32),
            pltpu.VMEM((RING, 2 * B, LANES), bf16),
            pltpu.SemaphoreType.DMA((RING,)),
            pltpu.SemaphoreType.DMA,
        ],
        compiler_params=params(16 + n // 4),
        cost_estimate=pl.CostEstimate(flops=4 * entries * 2 * B * LANES * LANES, bytes_accessed=16 << 20, transcendentals=0),
        name="far",
    )(me, meta, pin_hbm(left), pin(recv), pin_hbm(near_slots))

    def combine(first, count, parts):
        return pl.pallas_call(
            functools.partial(combine_kernel, n, cap, first, count),
            out_shape=[shape((count, TO, HALF, LANES), f32)] * 2,
            in_specs=[smem, smem] + [vmem] * PLACES,
            out_specs=[vmem] * 2,
            compiler_params=params(8 + n // 4),
            name="combine",
        )(me, table, *[pin(part) for part in parts])

    far_slots = [slots[0]] + [across(slots[j], lambda i, j=j: i ^ (2 * j)) for j in range(1, PLACES)]
    mine, other = combine(1, groups - 1, far_slots)
    got = across(other, lambda i: i ^ 1)
    parts = [
        across(mine[step - 1] + got[step - 1], lambda i, step=step: (i + step * GROUP) % n) for step in range(1, groups)
    ]
    own_slots = [slots[PLACES]] + [across(slots[PLACES + j], lambda i, j=j: i ^ (2 * j)) for j in range(1, PLACES)]
    mine, other = combine(0, 1, [part[None] for part in own_slots])
    parts += [mine[0], across(other, lambda i: i ^ 1)[0]]

    return pl.pallas_call(
        final_kernel,
        out_shape=jax.ShapeDtypeStruct((TO, B * B), f32),
        in_specs=[vmem] * len(parts),
        out_specs=vmem,
        scratch_shapes=[pltpu.VMEM((TO * HALF, LANES), f32)],
        compiler_params=params(8),
        name="final",
    )(*[pin(part) for part in parts])


def solution(mesh):
    in_specs = (
        P("elem", None, None),
        P("elem", None, None),
        P("elem", None),
        P("elem", None, None),
        P("elem"),
        P("elem", None),
        P("elem", None, None),
    )
    out_specs = P("elem", None)
    return jax.shard_map(body, mesh=mesh, in_specs=in_specs, out_specs=out_specs, check_vma=False)
```

time: 139 us -> 116 us (0.83)
  Pallas kernels: 65.2 us -> 43.8 us
  starting transfers between devices: 12.8 us -> 23.8 us
  local copies, waits for them, and re-layouts: 10.4 us -> 3.07 us
  waiting for transfers between devices: 48.2 us -> 42.7 us
    all_to_all x1 -> x0, waiting for transfers between devices: 48.2 us -> none  [body(): lax.all_to_all(send_two.reshape(n, cap * HALF, LANES), 'elem', split_axis...]
    ppermute x0 -> x14, waiting for transfers between devices: none -> 26.8 us  [across(): return lax.ppermute(value, 'elem', [(i, partner(i)) for i in range(n)])]
    ppermute x0 -> x14, starting transfers between devices: none -> 16.5 us  [across(): return lax.ppermute(value, 'elem', [(i, partner(i)) for i in range(n)])]
    all_to_all x1, waiting for transfers between devices: 0.03 us -> 15.9 us  [body(): lax.all_to_all(send.reshape(n, serve_count * B, LANES), 'elem', split_axi...]
    pallas_call x1, Pallas kernels: 42.5 us -> 29.2 us  [body(): pl.pallas_call(functools.partial(near_kernel, n), grid=(rows,), out_shape...]
    pallas_call x3 -> x5, Pallas kernels: 22.7 us -> 14.6 us  [the longest x1 8.52 us: body(): pl.pallas_call(functools.partial(far_kernel, n, cap), out_shape=slot_shap...]
    all_to_all x1 -> x0, starting transfers between devices: 5.53 us -> none  [body(): lax.all_to_all(send_two.reshape(n, cap * HALF, LANES), 'elem', split_axis...]
    unnamed x12 -> x7, local copies, waits for them, and re-layouts: 8.09 us -> 2.7 us
  transfers between devices with their start and end apart: 2 -> 15, of which waited for: 1 -> 10; matrix products, arithmetic and copies ran while one was open for 5% -> 3% of each run, Pallas kernels for 31% -> 26%
where the time goes in v1:
time: 116 us; the launch traced here: 114 us
  Pallas kernels  43.8 us (38%)
  waiting for transfers between devices  42.7 us (37%)
  starting transfers between devices  23.8 us (21%)
  local copies, waits for them, and re-layouts  3.07 us (3%)
    pallas_call x1, Pallas kernels, body(): pl.pallas_call(functools.partial(near_kernel, n), grid=(rows,), out_shape...  29.2 us
    ppermute x14, waiting for transfers between devices, across(): return lax.ppermute(value, 'elem', [(i, partner(i)) for i in range(n)])  26.8 us
    ppermute x14, starting transfers between devices, across(): return lax.ppermute(value, 'elem', [(i, partner(i)) for i in range(n)])  16.5 us
    all_to_all x1, waiting for transfers between devices, body(): lax.all_to_all(send.reshape(n, serve_count * B, LANES), 'elem', split_axi...  15.9 us
    pallas_call x1, Pallas kernels, body(): pl.pallas_call(functools.partial(far_kernel, n, cap), out_shape=slot_shap...  8.52 us
    all_to_all x1, starting transfers between devices, body(): lax.all_to_all(send.reshape(n, serve_count * B, LANES), 'elem', split_axi...  7.3 us
    pallas_call x1, Pallas kernels, body(): pl.pallas_call(functools.partial(prep_kernel, n), out_shape=(shape((rows,...  3.1 us
    unnamed x7, local copies, waits for them, and re-layouts  2.7 us
  transfers between devices with their start and end apart: 15, of which 10 were waited for; matrix products, arithmetic and copies ran while one was open for 3% of the time, Pallas kernels for 26%

profile of v1, /device:TPU:0, one launch (start us, length us, event | category | flops | bytes accessed | tf_op | source)
XLA Modules:
  0.0 114.2 jit_solution(10554862984591518807)
XLA Ops:
  0.0 3.1 %prep.1 = (f32[32,64,128]{2,1,0:T(8,128)S(1)}, f32[32,2,64,128]{3,2,1,0:T(8,128)}) custom-call(s32[1]{0:T(128)} %bitcast.me_ref, s32[2,31]{1,0:T(2,128)} %bitcast.50, f32[32,64,128]{2,1,0:T(8,128)} %bitcast.45), custom_call_target="tpu_custom_call" | custom-call | tf_op jit(solution)/shard_map/prep/pallas_call | solution.py:307
  3.1 7.3 %all-to-all-start = ((f32[32,128,128]{2,1,0:T(8,128)}), f32[32,128,128]{2,1,0:T(8,128)S(1)}, u32[]{:S(2)}, u32[]{:S(2)}) async-start(f32[32,128,128]{2,1,0:T(8,128)} %bitcast.44), calls=%async_computation | async-start | bytes 4194304 | tf_op jit(solution)/shard_map/all_to_all | solution.py:323
  10.4 2.7 %copy.12 = f32[28,8,32,128]{3,2,1,0:T(8,128)S(1)} copy(f32[28,8,32,128]{3,1,2,0:T(8,128)} %bitcast.43) | data formatting | bytes 7340032
  14.2 29.2 %near.1 = (bf16[224,128,128]{2,1,0:T(8,128)(2,1)}, f32[128,32,128]{2,1,0:T(8,128)}, s32[1856]{0:T(1024)S(1)}) custom-call(s32[1]{0:T(128)S(6)} %copy.13.count_row, s32[7,32]{1,0:T(8,128)S(1)} %bitcast.41, s32[32,28]{1,0:T(8,128)S(1)} %copy-done, s32[1]{0:T(128)} %bitcast.me_ref, f32[32,64,128]{2,1,0:T(8,128)S(1)} %get-tuple-element.22.own_ref, ...), custom_call_target="tpu_custom_call" | custom-call | flops 3758096384 | bytes 16777216 | tf_op jit(solution)/shard_map/near/pallas_call | solution.py:336
  43.4 15.9 %all-to-all-done = f32[32,128,128]{2,1,0:T(8,128)S(1)} async-done(((f32[32,128,128]{2,1,0:T(8,128)}), f32[32,128,128]{2,1,0:T(8,128)S(1)}, u32[]{:S(2)}, u32[]{:S(2)}) %all-to-all-start) | async-done | bytes 2097184 | tf_op jit(solution)/shard_map/all_to_all | solution.py:323
  59.3 8.5 %far.1 = (f32[3,2,4,32,128]{4,3,2,1,0:T(8,128)S(1)}, f32[3,2,4,32,128]{4,3,2,1,0:T(8,128)S(1)}, f32[3,2,4,32,128]{4,3,2,1,0:T(8,128)S(1)}, f32[3,2,4,32,128]{4,3...) custom-call(s32[1]{0:T(128)} %bitcast.me_ref, ...), custom_call_target="tpu_custom_call" | custom-call | flops 1879048192 | bytes 16777216 | tf_op jit(solution)/shard_map/far/pallas_call | solution.py:360
  67.8 2.5 %collective-permute-start.3 = (f32[3,2,4,32,128]{4,3,2,1,0:T(8,128)S(1)}, f32[3,2,4,32,128]{4,3,2,1,0:T(8,128)S(1)}, u32[]{:S(2)}, u32[]{:S(2)}) collective-permute-start(f32[3,2,4,32,128]{4,3,2,1,0:T(8,128)S(1)} %get-tuple-element.28), channel_id=1, source_target_pairs={{0,2},{1,3},{2,0},{3,1},{4,6},{5,7},{6,4},{7,5},{8,10},{9,11},{10,... | collective-permute-start | bytes 1179656 | tf_op jit(solution)/shard_map/ppermute | solution.py:304
  70.4 1.5 %collective-permute-start.5 = (f32[3,2,4,32,128]{4,3,2,1,0:T(8,128)S(1)}, f32[3,2,4,32,128]{4,3,2,1,0:T(8,128)S(1)}, u32[]{:S(2)}, u32[]{:S(2)}) collective-permute-start(f32[3,2,4,32,128]{4,3,2,1,0:T(8,128)S(1)} %get-tuple-element.30), channel_id=1, source_target_pairs={{0,6},{1,7},{2,4},{3,5},{4,2},{5,3},{6,0},{7,1},{8,14},{9,15},{10,... | collective-permute-start | bytes 1179656 | tf_op jit(solution)/shard_map/ppermute | solution.py:304
  73.1 1.3 %collective-permute-start.1 = (s32[2,4,32]{2,1,0:T(4,128)S(1)}, s32[2,4,32]{2,1,0:T(4,128)S(1)}, u32[]{:S(2)}, u32[]{:S(2)}) collective-permute-start(s32[2,4,32]{2,1,0:T(4,128)S(1)} %pad_add_fusion.2), channel_id=1, source_target_pairs={{0,8},{1,9},{2,10},{3,11},{4,12},{5,13},{6,14},{7,15},{8,0},{9,1},... | collective-permute-start | bytes 3080 | tf_op jit(solution)/shard_map/ppermute | solution.py:304
  74.4 2.3 %collective-permute-done.1 = s32[2,4,32]{2,1,0:T(4,128)S(1)} collective-permute-done((s32[2,4,32]{2,1,0:T(4,128)S(1)}, s32[2,4,32]{2,1,0:T(4,128)S(1)}, u32[]{:S(2)}, u32[]{:S(2)}) %collective-permute-start.1) | collective-permute-done | bytes 1056 | tf_op jit(solution)/shard_map/ppermute | solution.py:304
  76.7 1.6 %collective-permute-start.2 = (s32[4,4,32]{2,1,0:T(4,128)S(1)}, s32[4,4,32]{2,1,0:T(4,128)S(1)}, u32[]{:S(2)}, u32[]{:S(2)}) collective-permute-start(s32[4,4,32]{2,1,0:T(4,128)S(1)} %pad_add_fusion.1), channel_id=1, source_target_pairs={{0,16},{1,17},{2,18},{3,19},{4,20},{5,21},{6,22},{7,23},{8,24},{9,... | collective-permute-start | bytes 6152 | tf_op jit(solution)/shard_map/ppermute | solution.py:304
  78.3 3.0 %collective-permute-done.2 = s32[4,4,32]{2,1,0:T(4,128)S(1)} collective-permute-done((s32[4,4,32]{2,1,0:T(4,128)S(1)}, s32[4,4,32]{2,1,0:T(4,128)S(1)}, u32[]{:S(2)}, u32[]{:S(2)}) %collective-permute-start.2) | collective-permute-done | bytes 2080 | tf_op jit(solution)/shard_map/ppermute | solution.py:304
  81.3 5.5 %collective-permute-done.4.refs_2_ = f32[3,2,4,32,128]{4,3,2,1,0:T(8,128)S(1)} collective-permute-done((f32[3,2,4,32,128]{4,3,2,1,0:T(8,128)S(1)}, f32[3,2,4,32,128]{4,3,2,1,0:T(8,128)S(1)}, u32[]{:S(2)}, u32[]{:S(2)}) %collective-permute-start.4) | collective-permute-done | bytes 393248 | tf_op jit(solution)/shard_map/ppermute | solution.py:304
  86.7 1.8 %collective-permute-done.5.refs_3_ = f32[3,2,4,32,128]{4,3,2,1,0:T(8,128)S(1)} collective-permute-done((f32[3,2,4,32,128]{4,3,2,1,0:T(8,128)S(1)}, f32[3,2,4,32,128]{4,3,2,1,0:T(8,128)S(1)}, u32[]{:S(2)}, u32[]{:S(2)}) %collective-permute-start.5) | collective-permute-done | bytes 393248 | tf_op jit(solution)/shard_map/ppermute | solution.py:304
  88.5 1.2 %combine.2 = (f32[3,8,32,128]{3,2,1,0:T(8,128)S(1)}, f32[3,8,32,128]{3,2,1,0:T(8,128)S(1)}) custom-call(s32[1]{0:T(128)} %bitcast.me_ref, s32[32,32]{1,0:T(8,128)S(1)} %bitcast.33, f32[3,2,4,32,128]{4,3,2,1,0:T(8,128)S(1)} %get-tuple-element.27.refs_0_, f32[3,2,4,32,128]{4,3,2,1,0:T(8,128)S(1)} %collective-permute-done.3.refs_1_, ...), custom_call_target="tpu_custom_call" | custom-call | tf_op jit(solution)/shard_map/combine/pallas_call | solution.py:378
  90.5 1.7 %collective-permute-start.11 = (f32[2,4,32,128]{3,2,1,0:T(8,128)S(1)}, f32[2,4,32,128]{3,2,1,0:T(8,128)S(1)}, u32[]{:S(2)}, u32[]{:S(2)}) collective-permute-start(f32[2,4,32,128]{3,2,1,0:T(8,128)S(1)} %get-tuple-element.35), channel_id=1, source_target_pairs={{0,4},{1,5},{2,6},{3,7},{4,0},{5,1},{6,2},{7,3},{8,12},{9,13},{10,... | collective-permute-start | bytes 393224 | tf_op jit(solution)/shard_map/ppermute | solution.py:304
  92.3 1.2 %collective-permute-start.12 = (f32[2,4,32,128]{3,2,1,0:T(8,128)S(1)}, f32[2,4,32,128]{3,2,1,0:T(8,128)S(1)}, u32[]{:S(2)}, u32[]{:S(2)}) collective-permute-start(f32[2,4,32,128]{3,2,1,0:T(8,128)S(1)} %get-tuple-element.36), channel_id=1, source_target_pairs={{0,6},{1,7},{2,4},{3,5},{4,2},{5,3},{6,0},{7,1},{8,14},{9,15},{10,... | collective-permute-start | bytes 393224 | tf_op jit(solution)/shard_map/ppermute | solution.py:304
  93.4 2.8 %collective-permute-done.10 = f32[2,4,32,128]{3,2,1,0:T(8,128)S(1)} collective-permute-done((f32[2,4,32,128]{3,2,1,0:T(8,128)S(1)}, f32[2,4,32,128]{3,2,1,0:T(8,128)S(1)}, u32[]{:S(2)}, u32[]{:S(2)}) %collective-permute-start.10) | collective-permute-done | bytes 131104 | tf_op jit(solution)/shard_map/ppermute | solution.py:304
  96.2 2.7 %collective-permute-done.11 = f32[2,4,32,128]{3,2,1,0:T(8,128)S(1)} collective-permute-done((f32[2,4,32,128]{3,2,1,0:T(8,128)S(1)}, f32[2,4,32,128]{3,2,1,0:T(8,128)S(1)}, u32[]{:S(2)}, u32[]{:S(2)}) %collective-permute-start.11) | collective-permute-done | bytes 131104 | tf_op jit(solution)/shard_map/ppermute | solution.py:304
  100.0 1.4 %collective-permute-start.7 = (f32[8,32,128]{2,1,0:T(8,128)S(1)}, f32[8,32,128]{2,1,0:T(8,128)S(1)}, u32[]{:S(2)}, u32[]{:S(2)}) collective-permute-start(f32[8,32,128]{2,1,0:T(8,128)S(1)} %get-tuple-element.41), channel_id=1, source_target_pairs={{0,8},{1,9},{2,10},{3,11},{4,12},{5,13},{6,14},{7,15},{8,16},{9,17... | collective-permute-start | bytes 393224 | tf_op jit(solution)/shard_map/ppermute | solution.py:304
  101.4 2.2 %collective-permute-start.8 = (f32[8,32,128]{2,1,0:T(8,128)S(1)}, f32[8,32,128]{2,1,0:T(8,128)S(1)}, u32[]{:S(2)}, u32[]{:S(2)}) collective-permute-start(f32[8,32,128]{2,1,0:T(8,128)S(1)} %get-tuple-element.40), channel_id=1, source_target_pairs={{0,16},{1,17},{2,18},{3,19},{4,20},{5,21},{6,22},{7,23},{8,24},{9,... | collective-permute-start | bytes 393224 | tf_op jit(solution)/shard_map/ppermute | solution.py:304
  103.6 2.2 %collective-permute-start.9 = (f32[8,32,128]{2,1,0:T(8,128)S(1)}, f32[8,32,128]{2,1,0:T(8,128)S(1)}, u32[]{:S(2)}, u32[]{:S(2)}) collective-permute-start(f32[8,32,128]{2,1,0:T(8,128)S(1)} %get-tuple-element.39), channel_id=1, source_target_pairs={{0,24},{1,25},{2,26},{3,27},{4,28},{5,29},{6,30},{7,31},{8,0},{9,1... | collective-permute-start | bytes 393224 | tf_op jit(solution)/shard_map/ppermute | solution.py:304
  105.8 2.4 %collective-permute-done.7.refs_0_ = f32[8,32,128]{2,1,0:T(8,128)S(1)} collective-permute-done((f32[8,32,128]{2,1,0:T(8,128)S(1)}, f32[8,32,128]{2,1,0:T(8,128)S(1)}, u32[]{:S(2)}, u32[]{:S(2)}) %collective-permute-start.7) | collective-permute-done | bytes 131104 | tf_op jit(solution)/shard_map/ppermute | solution.py:304
  108.2 5.2 %collective-permute-done.8.refs_1_ = f32[8,32,128]{2,1,0:T(8,128)S(1)} collective-permute-done((f32[8,32,128]{2,1,0:T(8,128)S(1)}, f32[8,32,128]{2,1,0:T(8,128)S(1)}, u32[]{:S(2)}, u32[]{:S(2)}) %collective-permute-start.8) | collective-permute-done | bytes 131104 | tf_op jit(solution)/shard_map/ppermute | solution.py:304
  (24 shorter events, 4.1 us)
Async XLA Ops:
  3.1 56.2 %all-to-all-start = ((f32[32,128,128]{2,1,0:T(8,128)}), f32[32,128,128]{2,1,0:T(8,128)S(1)}, u32[]{:S(2)}, u32[]{:S(2)}) async-start(f32[32,128,128]{2,1,0:T(8,128)} %bitcast.44), calls=%async_computation | async-start | bytes 4194304 | tf_op jit(solution)/shard_map/all_to_all | solution.py:323
  13.1 1.1 copy-start
  13.1 1.1 copy-start.1
  59.3 12.6 %copy-start.2 = (s32[1,32,4]{1,2,0:T(4,128)S(1)}, s32[1,32,4]{1,2,0:T(4,128)}, u32[]{:S(2)}) copy-start(s32[1,32,4]{1,2,0:T(4,128)} %param.13) | copy-start | bytes 1540
  67.8 13.4 %collective-permute-start.3 = (f32[3,2,4,32,128]{4,3,2,1,0:T(8,128)S(1)}, f32[3,2,4,32,128]{4,3,2,1,0:T(8,128)S(1)}, u32[]{:S(2)}, u32[]{:S(2)}) collective-permute-start(f32[3,2,4,32,128]{4,3,2,1,0:T(8,128)S(1)} %get-tuple-element.28), channel_id=1, source_target_pairs={{0,2},{1,3},{2,0},{3,1},{4,6},{5,7},{6,4},{7,5},{8,10},{9,11},{10,... | collective-permute-start | bytes 1179656 | tf_op jit(solution)/shard_map/ppermute | solution.py:304
  70.4 16.4 %collective-permute-start.4 = (f32[3,2,4,32,128]{4,3,2,1,0:T(8,128)S(1)}, f32[3,2,4,32,128]{4,3,2,1,0:T(8,128)S(1)}, u32[]{:S(2)}, u32[]{:S(2)}) collective-permute-start(f32[3,2,4,32,128]{4,3,2,1,0:T(8,128)S(1)} %get-tuple-element.29), channel_id=1, source_target_pairs={{0,4},{1,5},{2,6},{3,7},{4,0},{5,1},{6,2},{7,3},{8,12},{9,13},{10,... | collective-permute-start | bytes 1179656 | tf_op jit(solution)/shard_map/ppermute | solution.py:304
  70.4 18.2 %collective-permute-start.5 = (f32[3,2,4,32,128]{4,3,2,1,0:T(8,128)S(1)}, f32[3,2,4,32,128]{4,3,2,1,0:T(8,128)S(1)}, u32[]{:S(2)}, u32[]{:S(2)}) collective-permute-start(f32[3,2,4,32,128]{4,3,2,1,0:T(8,128)S(1)} %get-tuple-element.30), channel_id=1, source_target_pairs={{0,6},{1,7},{2,4},{3,5},{4,2},{5,3},{6,0},{7,1},{8,14},{9,15},{10,... | collective-permute-start | bytes 1179656 | tf_op jit(solution)/shard_map/ppermute | solution.py:304
  71.9 1.2 %collective-permute-start = (s32[1,4,32]{2,1,0:T(4,128)S(1)}, s32[1,4,32]{2,1,0:T(4,128)S(1)}, u32[]{:S(2)}, u32[]{:S(2)}) collective-permute-start(s32[1,4,32]{2,1,0:T(4,128)S(1)} %bitcast.46), channel_id=1, source_target_pairs={{0,1},{1,0},{2,3},{3,2},{4,5},{5,4},{6,7},{7,6},{8,9},{9,8},{10,11... | collective-permute-start | bytes 1544 | tf_op jit(solution)/shard_map/ppermute | solution.py:304
  73.1 3.6 %collective-permute-start.1 = (s32[2,4,32]{2,1,0:T(4,128)S(1)}, s32[2,4,32]{2,1,0:T(4,128)S(1)}, u32[]{:S(2)}, u32[]{:S(2)}) collective-permute-start(s32[2,4,32]{2,1,0:T(4,128)S(1)} %pad_add_fusion.2), channel_id=1, source_target_pairs={{0,8},{1,9},{2,10},{3,11},{4,12},{5,13},{6,14},{7,15},{8,0},{9,1},... | collective-permute-start | bytes 3080 | tf_op jit(solution)/shard_map/ppermute | solution.py:304
  76.7 4.5 %collective-permute-start.2 = (s32[4,4,32]{2,1,0:T(4,128)S(1)}, s32[4,4,32]{2,1,0:T(4,128)S(1)}, u32[]{:S(2)}, u32[]{:S(2)}) collective-permute-start(s32[4,4,32]{2,1,0:T(4,128)S(1)} %pad_add_fusion.1), channel_id=1, source_target_pairs={{0,16},{1,17},{2,18},{3,19},{4,20},{5,21},{6,22},{7,23},{8,24},{9,... | collective-permute-start | bytes 6152 | tf_op jit(solution)/shard_map/ppermute | solution.py:304
  89.8 10.1 %collective-permute-start.6 = (f32[3,8,32,128]{3,2,1,0:T(8,128)S(1)}, f32[3,8,32,128]{3,2,1,0:T(8,128)S(1)}, u32[]{:S(2)}, u32[]{:S(2)}) collective-permute-start(f32[3,8,32,128]{3,2,1,0:T(8,128)S(1)} %get-tuple-element.32), channel_id=1, source_target_pairs={{0,1},{1,0},{2,3},{3,2},{4,5},{5,4},{6,7},{7,6},{8,9},{9,8},{10,11... | collective-permute-start | bytes 1179656 | tf_op jit(solution)/shard_map/ppermute | solution.py:304
  89.9 6.4 %collective-permute-start.10 = (f32[2,4,32,128]{3,2,1,0:T(8,128)S(1)}, f32[2,4,32,128]{3,2,1,0:T(8,128)S(1)}, u32[]{:S(2)}, u32[]{:S(2)}) collective-permute-start(f32[2,4,32,128]{3,2,1,0:T(8,128)S(1)} %get-tuple-element.34), channel_id=1, source_target_pairs={{0,2},{1,3},{2,0},{3,1},{4,6},{5,7},{6,4},{7,5},{8,10},{9,11},{10,... | collective-permute-start | bytes 393224 | tf_op jit(solution)/shard_map/ppermute | solution.py:304
  90.5 8.4 %collective-permute-start.11 = (f32[2,4,32,128]{3,2,1,0:T(8,128)S(1)}, f32[2,4,32,128]{3,2,1,0:T(8,128)S(1)}, u32[]{:S(2)}, u32[]{:S(2)}) collective-permute-start(f32[2,4,32,128]{3,2,1,0:T(8,128)S(1)} %get-tuple-element.35), channel_id=1, source_target_pairs={{0,4},{1,5},{2,6},{3,7},{4,0},{5,1},{6,2},{7,3},{8,12},{9,13},{10,... | collective-permute-start | bytes 393224 | tf_op jit(solution)/shard_map/ppermute | solution.py:304
  92.3 6.6 %collective-permute-start.12 = (f32[2,4,32,128]{3,2,1,0:T(8,128)S(1)}, f32[2,4,32,128]{3,2,1,0:T(8,128)S(1)}, u32[]{:S(2)}, u32[]{:S(2)}) collective-permute-start(f32[2,4,32,128]{3,2,1,0:T(8,128)S(1)} %get-tuple-element.36), channel_id=1, source_target_pairs={{0,6},{1,7},{2,4},{3,5},{4,2},{5,3},{6,0},{7,1},{8,14},{9,15},{10,... | collective-permute-start | bytes 393224 | tf_op jit(solution)/shard_map/ppermute | solution.py:304
  99.8 6.0 %collective-permute-start.13 = (f32[1,8,32,128]{3,2,1,0:T(8,128)S(1)}, f32[1,8,32,128]{3,2,1,0:T(8,128)S(1)}, u32[]{:S(2)}, u32[]{:S(2)}) collective-permute-start(f32[1,8,32,128]{3,2,1,0:T(8,128)S(1)} %get-tuple-element.38), channel_id=1, source_target_pairs={{0,1},{1,0},{2,3},{3,2},{4,5},{5,4},{6,7},{7,6},{8,9},{9,8},{10,11... | collective-permute-start | bytes 393224 | tf_op jit(solution)/shard_map/ppermute | solution.py:304
  100.0 8.2 %collective-permute-start.7 = (f32[8,32,128]{2,1,0:T(8,128)S(1)}, f32[8,32,128]{2,1,0:T(8,128)S(1)}, u32[]{:S(2)}, u32[]{:S(2)}) collective-permute-start(f32[8,32,128]{2,1,0:T(8,128)S(1)} %get-tuple-element.41), channel_id=1, source_target_pairs={{0,8},{1,9},{2,10},{3,11},{4,12},{5,13},{6,14},{7,15},{8,16},{9,17... | collective-permute-start | bytes 393224 | tf_op jit(solution)/shard_map/ppermute | solution.py:304
  101.4 12.0 %collective-permute-start.8 = (f32[8,32,128]{2,1,0:T(8,128)S(1)}, f32[8,32,128]{2,1,0:T(8,128)S(1)}, u32[]{:S(2)}, u32[]{:S(2)}) collective-permute-start(f32[8,32,128]{2,1,0:T(8,128)S(1)} %get-tuple-element.40), channel_id=1, source_target_pairs={{0,16},{1,17},{2,18},{3,19},{4,20},{5,21},{6,22},{7,23},{8,24},{9,... | collective-permute-start | bytes 393224 | tf_op jit(solution)/shard_map/ppermute | solution.py:304
  103.6 9.8 %collective-permute-start.9 = (f32[8,32,128]{2,1,0:T(8,128)S(1)}, f32[8,32,128]{2,1,0:T(8,128)S(1)}, u32[]{:S(2)}, u32[]{:S(2)}) collective-permute-start(f32[8,32,128]{2,1,0:T(8,128)S(1)} %get-tuple-element.39), channel_id=1, source_target_pairs={{0,24},{1,25},{2,26},{3,27},{4,28},{5,29},{6,30},{7,31},{8,0},{9,1... | collective-permute-start | bytes 393224 | tf_op jit(solution)/shard_map/ppermute | solution.py:304
